TPU v7x, 32 devices: a whole 2x2x4 slice. The times are simulated.
32 devices in a mesh: ctx: 16 (over z, y, core), head: 2 (over x).
Axes of the slice: x: 2, y: 2, z: 4, core: 2. Of those that a mesh axis runs over, the one named last changes fastest.
Arguments:
- q_nope: bfloat16 [1024, 8192], P('ctx', 'head'), may hold values from -6 to 6
- query_rope: bfloat16 [1024, 4096], P('ctx', 'head'), may hold values from -80 to 80
- latent: bfloat16 [1024, 512], P('ctx'), may hold values from -6 to 6
- key_rope: bfloat16 [1024, 64], P('ctx'), may hold values from -3 to 3
- w_uk: bfloat16 [64, 128, 512], P('head'), may hold values from -0.5 to 0.5
- w_uv: bfloat16 [64, 512, 128], P('head'), may hold values from -1 to 1
- w_out: bfloat16 [64, 128, 3584], P('head', None, 'ctx'), may hold values from -0.0625 to 0.0625
Outputs:
- mixed: bfloat16 [1024, 3584], P(('ctx', 'head'))
All inputs are finite; a program needn't handle non-finite values.
Results may differ from a plain program's by a relative error of at most 0.015.
Values may be sent and summed in bfloat16 or wider, within the bound.
A program may use at most 128 MiB of HBM per device.

v0:
```python
import jax
import jax.numpy as jnp
from jax import lax
from jax.sharding import PartitionSpec as P

NOPE = 128
ROPE = 64


def folded_position(row_ids, shard_rows, shard_count):
    half_len = shard_rows // 2
    block_index = row_ids // shard_rows
    within_block = row_ids % shard_rows
    return jnp.where(
        within_block < half_len,
        block_index * half_len + within_block,
        (2 * shard_count - 1 - block_index) * half_len + within_block - half_len,
    )


def attend_block(
    state_now, lat_block, rope_block, pos_block, query_latent, query_rope, query_pos, score_scale
):
    best_now, total_now, accum_now = state_now
    scores = jnp.einsum(
        "qhl,kl->qhk", query_latent, lat_block, preferred_element_type=jnp.float32
    ) + jnp.einsum("qhr,kr->qhk", query_rope, rope_block, preferred_element_type=jnp.float32)
    scores = scores * score_scale
    visible = pos_block[None, None, :] <= query_pos[:, None, None]
    block_best = jnp.max(jnp.where(visible, scores, -jnp.inf), axis=2)
    best_next = jnp.maximum(best_now, block_best)
    weights = jnp.where(visible, jnp.exp(scores - best_next[:, :, None]), 0.0)
    factor = jnp.exp(best_now - best_next)
    total_next = total_now * factor + jnp.sum(weights, axis=2)
    accum_next = accum_now * factor[:, :, None] + jnp.einsum(
        "qhk,kl->qhl", weights.astype(jnp.bfloat16), lat_block, preferred_element_type=jnp.float32
    )
    return (best_next, total_next, accum_next)


def make_fold(query_latent, query_rope, query_pos, row_map, score_scale):

    def fold_keys(state_now, key_piece, row_start):
        lat_piece, rope_piece = key_piece
        key_count = lat_piece.shape[0]
        block_len = key_count
        while block_len > 512 and block_len % 2 == 0:
            block_len = block_len // 2
        blocks = key_count // block_len
        key_pos = row_map(jnp.arange(key_count, dtype=jnp.int32))

        def scan_step(state_inner, block_items):
            lat_block, rope_block, pos_block = block_items
            return (
                attend_block(
                    state_inner,
                    lat_block,
                    rope_block,
                    pos_block,
                    query_latent,
                    query_rope,
                    query_pos,
                    score_scale,
                ),
                None,
            )

        state_out, unused = lax.scan(
            scan_step,
            state_now,
            (
                lat_piece.reshape(blocks, block_len, lat_piece.shape[1]),
                rope_piece.reshape(blocks, block_len, rope_piece.shape[1]),
                key_pos.reshape(blocks, block_len),
            ),
        )
        return state_out

    return fold_keys


def shards(q_nope, query_rope, latent, key_rope, w_uk, w_uv, w_out):
    shard_rows = latent.shape[0]
    shard_count = lax.axis_size("ctx")
    heads_here = w_uk.shape[0]
    score_scale = (NOPE + ROPE) ** (-0.5)
    nope_part = q_nope.reshape(shard_rows, heads_here, NOPE)
    query_latent = jnp.einsum(
        "qhn,hnl->qhl", nope_part, w_uk, preferred_element_type=jnp.float32
    ).astype(jnp.bfloat16)
    rope_part = query_rope.reshape(shard_rows, heads_here, ROPE)
    own_rows = lax.axis_index("ctx") * shard_rows + jnp.arange(shard_rows, dtype=jnp.int32)
    query_pos = folded_position(own_rows, shard_rows, shard_count)
    initial = (
        jnp.full((shard_rows, heads_here), -1e30, jnp.float32),
        jnp.zeros((shard_rows, heads_here), jnp.float32),
        jnp.zeros((shard_rows, heads_here, latent.shape[1]), jnp.float32),
    )

    def direct_map(row_ids):
        return folded_position(row_ids, shard_rows, shard_count)

    fold_keys = make_fold(query_latent, rope_part, query_pos, direct_map, score_scale)
    final_state = fold_keys(
        initial,
        (
            lax.all_gather(latent, "ctx", axis=0, tiled=True),
            lax.all_gather(key_rope, "ctx", axis=0, tiled=True),
        ),
        jnp.int32(0),
    )
    best_state, total_state, accum_state = final_state
    latent_out = (accum_state / total_state[:, :, None]).astype(jnp.bfloat16)
    head_out = jnp.einsum(
        "qhl,hlv->qhv", latent_out, w_uv, preferred_element_type=jnp.float32
    ).astype(jnp.bfloat16)
    partial_sum = jnp.einsum(
        "qhv,hvd->qd",
        head_out,
        lax.all_gather(w_out, "ctx", axis=2, tiled=True),
        preferred_element_type=jnp.float32,
    )
    mixed = lax.psum_scatter(
        partial_sum.astype(jnp.bfloat16), "head", scatter_dimension=0, tiled=True
    )
    return mixed


def solution(mesh):
    placed = (
        P("ctx", "head"),
        P("ctx", "head"),
        P("ctx", None),
        P("ctx", None),
        P("head", None, None),
        P("head", None, None),
        P("head", None, "ctx"),
    )
    return jax.shard_map(
        shards, mesh=mesh, in_specs=placed, out_specs=P(("ctx", "head"), None), check_vma=False
    )
```

profile of v0, /device:TPU:0, one launch (start us, length us, event | category | flops | bytes accessed | tf_op | source)
XLA Modules:
  0.0 237.0 jit_solution(16369758039684738673)
XLA Ops:
  6.5 0.0 copy-start
  6.5 0.0 all-gather.3.cloned.1.call-start
  6.5 0.7 all-gather.3.cloned.1.call-update
  7.3 0.0 all-gather.5.cloned.1.call-start
  7.3 0.7 all-gather.5.cloned.1.call-update
  8.0 0.0 reduce-scatter.2.cloned.1.call-start
  8.1 1.5 reshape.58
  9.6 0.2 copy.17
  9.8 24.3 %all_gather.10 = bf16[1024,64]{1,0:T(8,128)(2,1)S(1)} all-gather(bf16[64,64]{1,0:T(8,128)(2,1)} %param.12), channel_id=1, replica_groups=mesh['ctx'=16,'head'=2] {'ctx'}, dimensions={0}, use_global_device_ids=true | all-gather | bytes 139264 | tf_op jit(solution)/shard_map/all_gather | solution.py:108
  34.1 0.1 copy.16
  34.3 0.0 copy-done
  34.3 4.3 %convert_bitcast_fusion = bf16[64,32,512]{2,0,1:T(8,128)(2,1)} fusion(bf16[32,128,512]{2,1,0:T(8,128)(2,1)} %param.13, bf16[64,4096]{1,0:T(8,128)(2,1)S(1)} %copy-done), kind=kOutput, calls=%fused_computation.39 | convolution fusion | flops 269484032 | bytes 6815744 | tf_op jit(solution)/shard_map/qhn,hnl->qhl/dot_general | solution.py:88
  38.5 11.7 %all-gather.3.cloned.1.call-done = bf16[1024,512]{1,0:T(8,128)(2,1)} async-done(((bf16[64,512]{1,0:T(8,128)(2,1)}), bf16[1024,512]{1,0:T(8,128)(2,1)}) %all-gather.3.cloned.1.call-update) | async-done | bytes 1048592 | tf_op jit(solution)/shard_map/all_gather | solution.py:107
  50.3 32.0 %while.15 = (s32[]{:T(128)}, f32[64,32]{0,1:T(8,128)S(1)}, f32[64,32]{0,1:T(8,128)S(1)}, f32[64,32,512]{2,1,0:T(8,128)}, s32[2,512]{1,0:T(2,128)S(1)}, /*index=5...) while((s32[]{:T(128)}, f32[64,32]{0,1:T(8,128)S(1)}, ...), condition=%wide.region_3.4_spmd.clone, body=%wide.region_0.3_spmd.clone.sunk | while | flops 2293280512 | bytes 33341068 | solution.py:68
  50.3 3.1 %fusion.54 = f32[512,64,32]{0,1,2:T(8,128)S(1)} fusion(bf16[64,32,512]{2,0,1:T(8,128)(2,1)} %get-tuple-element.235, bf16[2,512,512]{2,1,0:T(8,128)(2,1)} %get-tuple-element.234, s32[]{:T(128)} %get-tuple-element.217), kind=kOutput, calls=%fused_computation.13.clone.1 | convolution fusion | flops 1073741824 | bytes 6816256 | tf_op jit(solution)/shard_map/while/body/eval_jaxpr/qhl,kl->qhk/dot_general | solution.py:25
  53.4 0.1 broadcast_compare_fusion.2
  53.5 2.9 %fusion.55 = (f32[64,32]{0,1:T(8,128)S(1)}, f32[512,64,32]{0,1,2:T(8,128)}) fusion(pred[64,512]{1,0:T(8,128)(4,1)S(1)} %broadcast_compare_fusion.2, f32[512,64,32]{0,1,2:T(8,128)S(1)} %fusion.54, bf16[64,32,64]{2,0,1:T(8,128)(2,1)S(1)} %get-tuple-element.237, bf16[2,512,64]{1,2,0:T(8,128)(2,1)S(1)} %get-tuple-element.236, s32[]{:T(128)} %get-tuple-element.217), kind=kOutput, calls=%fused_computation.3.clone.1 | convolution fusion | flops 138409984 | bytes 9019396 | tf_op jit(solution)/shard_map/while/body/eval_jaxpr/qhr,kr->qhk/dot_general | solution.py:27
  56.4 4.6 %fusion.56 = (bf16[64,32,512]{2,0,1:T(8,128)(2,1)S(1)}, f32[64,32]{0,1:T(8,128)S(1)}) fusion(f32[512,64,32]{0,1,2:T(8,128)} %get-tuple-element.200, f32[64,32]{0,1:T(8,128)S(1)} %select_maximum_fusion.2, pred[64,512]{1,0:T(8,128)(4,1)S(1)} %broadcast_compare_fusion.2), kind=kLoop, calls=%fused_computation.9.clone.1 | loop fusion | flops 4192256 | bytes 6340608 | tf_op jit(solution)/shard_map/while/body/eval_jaxpr/convert_element_type | solution.py:36
  61.1 0.1 copy.40
  61.2 5.0 %fusion.58 = f32[64,32,512]{2,1,0:T(8,128)} fusion(f32[64,32,512]{2,1,0:T(8,128)} %get-tuple-element.220, bf16[64,32,512]{2,0,1:T(8,128)(2,1)S(1)} %get-tuple-element.203, f32[64,32]{1,0:T(8,128)S(1)} %copy.40, pred[]{:T(512)S(6)} %compare.11, bf16[2,512,512]{2,1,0:T(8,128)(2,1)} %get-tuple-element.234, s32[]{:T(128)} %get-tuple-element.217), kind=kOutput, calls=%fused_computation.7.clone.1 | convolution fusion | flops 1076887552 | bytes 11018753 | tf_op jit(solution)/shard_map/while/body/eval_jaxpr/qhk,kl->qhl/dot_general | solution.py:35
  66.1 3.1 %fusion.54 = f32[512,64,32]{0,1,2:T(8,128)S(1)} fusion(bf16[64,32,512]{2,0,1:T(8,128)(2,1)} %get-tuple-element.235, bf16[2,512,512]{2,1,0:T(8,128)(2,1)} %get-tuple-element.234, s32[]{:T(128)} %get-tuple-element.217), kind=kOutput, calls=%fused_computation.13.clone.1 | convolution fusion | flops 1073741824 | bytes 6816256 | tf_op jit(solution)/shard_map/while/body/eval_jaxpr/qhl,kl->qhk/dot_general | solution.py:25
  69.3 0.1 broadcast_compare_fusion.2
  69.4 2.9 %fusion.55 = (f32[64,32]{0,1:T(8,128)S(1)}, f32[512,64,32]{0,1,2:T(8,128)}) fusion(pred[64,512]{1,0:T(8,128)(4,1)S(1)} %broadcast_compare_fusion.2, f32[512,64,32]{0,1,2:T(8,128)S(1)} %fusion.54, bf16[64,32,64]{2,0,1:T(8,128)(2,1)S(1)} %get-tuple-element.237, bf16[2,512,64]{1,2,0:T(8,128)(2,1)S(1)} %get-tuple-element.236, s32[]{:T(128)} %get-tuple-element.217), kind=kOutput, calls=%fused_computation.3.clone.1 | convolution fusion | flops 138409984 | bytes 9019396 | tf_op jit(solution)/shard_map/while/body/eval_jaxpr/qhr,kr->qhk/dot_general | solution.py:27
  72.3 3.5 %fusion.56 = (bf16[64,32,512]{2,0,1:T(8,128)(2,1)S(1)}, f32[64,32]{0,1:T(8,128)S(1)}) fusion(f32[512,64,32]{0,1,2:T(8,128)} %get-tuple-element.200, f32[64,32]{0,1:T(8,128)S(1)} %select_maximum_fusion.2, pred[64,512]{1,0:T(8,128)(4,1)S(1)} %broadcast_compare_fusion.2), kind=kLoop, calls=%fused_computation.9.clone.1 | loop fusion | flops 4192256 | bytes 6340608 | tf_op jit(solution)/shard_map/while/body/eval_jaxpr/convert_element_type | solution.py:36
  75.8 0.1 copy.40
  75.9 6.4 %fusion.58 = f32[64,32,512]{2,1,0:T(8,128)} fusion(f32[64,32,512]{2,1,0:T(8,128)} %get-tuple-element.220, bf16[64,32,512]{2,0,1:T(8,128)(2,1)S(1)} %get-tuple-element.203, f32[64,32]{1,0:T(8,128)S(1)} %copy.40, pred[]{:T(512)S(6)} %compare.11, bf16[2,512,512]{2,1,0:T(8,128)(2,1)} %get-tuple-element.234, s32[]{:T(128)} %get-tuple-element.217), kind=kOutput, calls=%fused_computation.7.clone.1 | convolution fusion | flops 1076887552 | bytes 11018753 | tf_op jit(solution)/shard_map/while/body/eval_jaxpr/qhk,kl->qhl/dot_general | solution.py:35
  82.3 0.1 copy.18
  82.4 2.6 %divide_convert_fusion = bf16[64,32,512]{2,1,0:T(8,128)(2,1)S(1)} fusion(f32[64,32,512]{2,1,0:T(8,128)} %get-tuple-element.58, f32[64,32]{1,0:T(8,128)S(1)} %copy.18), kind=kLoop, calls=%fused_computation.36 | loop fusion | flops 2097152 | bytes 6299648 | tf_op jit(solution)/shard_map/convert_element_type | solution.py:113
  84.9 114.2 %all-gather.5.cloned.1.call-done = bf16[32,128,3584]{1,2,0:T(8,128)(2,1)} async-done(((bf16[32,128,224]{1,2,0:T(8,128)(2,1)}), bf16[32,128,3584]{1,2,0:T(8,128)(2,1)}) %all-gather.5.cloned.1.call-update) | async-done | bytes 29360144 | tf_op jit(solution)/shard_map/all_gather | solution.py:120
  199.1 17.4 %fusion.20 = bf16[64,3584]{1,0:T(8,128)(2,1)} fusion(bf16[32,128,3584]{1,2,0:T(8,128)(2,1)} %all-gather.5.cloned.1.call-done, bf16[32,512,128]{2,1,0:T(8,128)(2,1)} %param.14, bf16[64,32,512]{2,1,0:T(8,128)(2,1)S(1)} %divide_convert_fusion), kind=kOutput, calls=%fused_computation.35 | convolution fusion | flops 2147975168 | bytes 36110336 | tf_op jit(solution)/shard_map/qhv,hvd->qd/dot_general | solution.py:117
  216.5 0.0 reduce-scatter.2.cloned.1.call-update
  216.5 14.0 %reduce-scatter.2.cloned.1.call-done = bf16[32,3584]{1,0:T(8,128)(2,1)} async-done(((bf16[64,3584]{1,0:T(8,128)(2,1)}), bf16[32,3584]{1,0:T(8,128)(2,1)}) %reduce-scatter.2.cloned.1.call-update) | async-done | bytes 229392 | tf_op jit(solution)/shard_map/reduce_scatter | solution.py:123
  (14 shorter events, 0.1 us)
Async XLA Ops:
  6.5 27.7 %copy-start = (bf16[64,4096]{1,0:T(8,128)(2,1)S(1)}, bf16[64,4096]{1,0:T(8,128)(2,1)}, u32[]{:S(2)}) copy-start(bf16[64,4096]{1,0:T(8,128)(2,1)} %param.9) | copy-start | bytes 1572868
  6.5 43.7 %all-gather.3.cloned.1.call-start = ((), (), s32[]{:S(2)}) async-start(), calls=%async_computation.1 | async-start | bytes 1114112 | tf_op jit(solution)/shard_map/all_gather | solution.py:107
  7.3 191.8 %all-gather.5.cloned.1.call-start = ((), (), s32[]{:S(2)}) async-start(), calls=%async_computation.2 | async-start | bytes 31195136 | tf_op jit(solution)/shard_map/all_gather | solution.py:120
  8.0 222.5 %reduce-scatter.2.cloned.1.call-start = ((), (), s32[]{:S(2)}) async-start(), calls=%async_computation.3 | async-start | bytes 688128 | tf_op jit(solution)/shard_map/reduce_scatter | solution.py:123
Sparse Core Ops, SparseCore 0:
  9.5 40.7 all-gather.2
  51.8 147.2 all-gather.4
  216.6 13.8 reduce-scatter.1
where the time goes:
time: 237 us
  waiting for transfers between devices  141 us (59%)
  matrix products  45 us (19%)
  blocking collectives  24.3 us (10%)
  between operations  13.2 us (6%)
  other arithmetic  10.9 us (5%)
    all_gather x1, waiting for transfers between devices, shards(): lax.all_gather(w_out, 'ctx', axis=2, tiled=True)  114 us
    all_gather x1, blocking collectives, shards(): lax.all_gather(key_rope, 'ctx', axis=0, tiled=True)  24.3 us
    dot_general x1, matrix products, shards(): jnp.einsum('qhv,hvd->qd', head_out, lax.all_gather(w_out, 'ctx', axis=2,...  17.4 us
    reduce_scatter x1, waiting for transfers between devices, shards(): lax.psum_scatter(partial_sum.astype(jnp.bfloat16), 'head', scatter_dimens...  14 us
    all_gather x1, waiting for transfers between devices, shards(): lax.all_gather(latent, 'ctx', axis=0, tiled=True)  11.7 us
    dot_general x2, matrix products, attend_block(): jnp.einsum('qhk,kl->qhl', weights.astype(jnp.bfloat16), lat_block, prefer...  11.4 us
    convert_element_type x2, other arithmetic, attend_block(): weights.astype(jnp.bfloat16)  8.09 us
    dot_general x2, matrix products, attend_block(): jnp.einsum('qhl,kl->qhk', query_latent, lat_block, preferred_element_type...  6.15 us
  transfers between devices with their start and end apart: 3, of which 3 were waited for; matrix products, arithmetic and copies ran while one was open for 17% of the time, Pallas kernels for 0%

commit v1 on v0

--- a/solution.py
+++ b/solution.py
@@ -100,12 +100,13 @@
     def direct_map(row_ids):
         return folded_position(row_ids, shard_rows, shard_count)
 
+    keys_all = lax.all_gather(jnp.concatenate([latent, key_rope], axis=1), "ctx", axis=0, tiled=True)
     fold_keys = make_fold(query_latent, rope_part, query_pos, direct_map, score_scale)
     final_state = fold_keys(
         initial,
         (
-            lax.all_gather(latent, "ctx", axis=0, tiled=True),
-            lax.all_gather(key_rope, "ctx", axis=0, tiled=True),
+            keys_all[:, : latent.shape[1]],
+            keys_all[:, latent.shape[1] :],
         ),
         jnp.int32(0),
     )
@@ -114,15 +115,19 @@
     head_out = jnp.einsum(
         "qhl,hlv->qhv", latent_out, w_uv, preferred_element_type=jnp.float32
     ).astype(jnp.bfloat16)
+    heads_all = lax.all_gather(head_out.reshape(shard_rows, -1), "ctx", axis=0, tiled=True)
     partial_sum = jnp.einsum(
-        "qhv,hvd->qd",
-        head_out,
-        lax.all_gather(w_out, "ctx", axis=2, tiled=True),
+        "qk,kd->qd",
+        heads_all,
+        w_out.reshape(-1, w_out.shape[2]),
         preferred_element_type=jnp.float32,
-    )
-    mixed = lax.psum_scatter(
-        partial_sum.astype(jnp.bfloat16), "head", scatter_dimension=0, tiled=True
-    )
+    ).astype(jnp.bfloat16)
+    head_count = lax.axis_size("head")
+    own_rows = shard_rows // head_count
+    by_owner = partial_sum.reshape(shard_count, head_count, own_rows, w_out.shape[2])
+    summed = lax.psum_scatter(by_owner, "head", scatter_dimension=1, tiled=True)
+    swapped = lax.all_to_all(summed[:, 0], "ctx", split_axis=0, concat_axis=0, tiled=True)
+    mixed = swapped.transpose(1, 0, 2).reshape(own_rows, shard_count * w_out.shape[2])
     return mixed
 
 

time: 237 us -> 228 us (0.962)
  local copies, waits for them, and re-layouts: 2.08 us -> 11.1 us
  blocking collectives: 24.3 us -> 15.5 us
  matrix products: 45 us -> 36.9 us
  waiting for transfers between devices: 141 us -> 137 us
  other arithmetic: 10.9 us -> 14 us
    unnamed x3 -> x4, waiting for transfers between devices: 1.42 us -> 26.5 us
    all_gather x1 -> x0, blocking collectives: 24.3 us -> none  [shards(): lax.all_gather(key_rope, 'ctx', axis=0, tiled=True)]
    all_gather x2, waiting for transfers between devices: 126 us -> 110 us  [the longest x1 73.6 us: shards(): lax.all_gather(head_out.reshape(shard_rows, -1), 'ctx', axis=0, tiled=True)]
    all_to_all x0 -> x1, blocking collectives: none -> 15.5 us  [shards(): lax.all_to_all(summed[:, 0], 'ctx', split_axis=0, concat_axis=0, tiled=True)]
    reduce_scatter x1 -> x0, waiting for transfers between devices: 14 us -> none  [shards(): lax.psum_scatter(partial_sum.astype(jnp.bfloat16), 'head', scatter_dimens...]
    dot_general x1 -> x2, matrix products: 17.4 us -> 8.54 us  [the longest x1 6.02 us: shards(): jnp.einsum('qk,kd->qd', heads_all, w_out.reshape(-1, w_out.shape[2]), pre...]
  transfers between devices with their start and end apart: 3 -> 3, of which waited for: 3 -> 3; matrix products, arithmetic and copies ran while one was open for 17% -> 3% of each run, Pallas kernels for 0% -> 0%
where the time goes in v1:
time: 228 us
  waiting for transfers between devices  137 us (60%)
  matrix products  36.9 us (16%)
  blocking collectives  15.5 us (7%)
  other arithmetic  14 us (6%)
  between operations  13.2 us (6%)
  local copies, waits for them, and re-layouts  11.1 us (5%)
    all_gather x1, waiting for transfers between devices, shards(): lax.all_gather(head_out.reshape(shard_rows, -1), 'ctx', axis=0, tiled=True)  73.6 us
    all_gather x1, waiting for transfers between devices, shards(): lax.all_gather(jnp.concatenate([latent, key_rope], axis=1), 'ctx', axis=0...  36.7 us
    unnamed x4, waiting for transfers between devices  26.5 us
    all_to_all x1, blocking collectives, shards(): lax.all_to_all(summed[:, 0], 'ctx', split_axis=0, concat_axis=0, tiled=True)  15.5 us
    dot_general x2, matrix products, attend_block(): jnp.einsum('qhk,kl->qhl', weights.astype(jnp.bfloat16), lat_block, prefer...  12.4 us
    convert_element_type x2, other arithmetic, attend_block(): weights.astype(jnp.bfloat16)  9.39 us
    dot_general x1, matrix products, shards(): jnp.einsum('qk,kd->qd', heads_all, w_out.reshape(-1, w_out.shape[2]), pre...  6.02 us
    dot_general x2, matrix products, attend_block(): jnp.einsum('qhl,kl->qhk', query_latent, lat_block, preferred_element_type...  5.82 us
  transfers between devices with their start and end apart: 3, of which 3 were waited for; matrix products, arithmetic and copies ran while one was open for 3% of the time, Pallas kernels for 0%

profile of v1, /device:TPU:0, one launch (start us, length us, event | category | flops | bytes accessed | tf_op | source)
XLA Modules:
  0.0 227.8 jit_solution(13986669128928047919)
XLA Ops:
  6.5 0.0 copy-start
  6.5 0.0 all-gather.3.cloned.1.call-start
  6.5 1.6 pad_maximum_fusion
  8.2 0.0 all-gather.3.cloned.1.call-update
  8.2 0.0 all-gather.5.cloned.1.call-start
  8.3 1.5 reshape.70
  9.7 0.2 copy.42
  10.0 4.4 %convert_bitcast_fusion = bf16[64,32,512]{2,0,1:T(8,128)(2,1)} fusion(bf16[32,128,512]{2,1,0:T(8,128)(2,1)} %param.13, bf16[64,4096]{1,0:T(8,128)(2,1)} %param.9), kind=kOutput, calls=%fused_computation.37 | convolution fusion | flops 269484032 | bytes 6815744 | tf_op jit(solution)/shard_map/qhn,hnl->qhl/dot_general | solution.py:88
  14.4 36.7 %all-gather.3.cloned.1.call-done = bf16[1024,576]{1,0:T(8,128)(2,1)} async-done(((bf16[64,576]{1,0:T(8,128)(2,1)}), bf16[1024,576]{1,0:T(8,128)(2,1)}) %all-gather.3.cloned.1.call-update) | async-done | bytes 1179664 | tf_op jit(solution)/shard_map/all_gather | solution.py:103
  51.2 1.0 slice.9
  52.1 0.8 copy.41
  52.9 1.3 slice.8
  54.2 33.8 %while.15 = (s32[]{:T(128)}, f32[64,32]{0,1:T(8,128)S(1)}, f32[64,32]{0,1:T(8,128)S(1)}, f32[64,32,512]{2,1,0:T(8,128)}, s32[2,512]{1,0:T(2,128)S(1)}, /*index=5...) while((s32[]{:T(128)}, f32[64,32]{0,1:T(8,128)S(1)}, ...), condition=%wide.region_3.4_spmd.clone, body=%wide.region_0.3_spmd.clone.sunk | while | flops 2293280512 | bytes 33888944 | solution.py:68
  54.2 0.0 copy-start.2
  54.3 2.9 %fusion.58 = f32[512,64,32]{0,1,2:T(8,128)S(1)} fusion(bf16[64,32,512]{2,0,1:T(8,128)(2,1)} %get-tuple-element.255, bf16[2,512,512]{2,1,0:T(8,128)(2,1)S(1)} %get-tuple-element.254, s32[]{:T(128)} %get-tuple-element.237), kind=kOutput, calls=%fused_computation.13.clone.1 | convolution fusion | flops 1073741824 | bytes 6815748 | tf_op jit(solution)/shard_map/while/body/eval_jaxpr/qhl,kl->qhk/dot_general | solution.py:25
  57.2 0.1 broadcast_compare_fusion.2
  57.3 0.0 copy-done.2
  57.3 2.9 %fusion.59 = (f32[64,32]{0,1:T(8,128)S(1)}, f32[512,64,32]{0,1,2:T(8,128)}) fusion(pred[64,512]{1,0:T(8,128)(4,1)S(1)} %broadcast_compare_fusion.2, f32[512,64,32]{0,1,2:T(8,128)S(1)} %fusion.58, bf16[64,32,64]{2,0,1:T(8,128)(2,1)S(1)} %get-tuple-element.257, bf16[2,512,64]{1,2,0:T(8,128)(2,1)S(1)} %copy-done.2, s32[]{:T(128)} %get-tuple-element.237), kind=kOutput, calls=%fused_computation.3.clone.1 | convolution fusion | flops 138409984 | bytes 9019396 | tf_op jit(solution)/shard_map/while/body/eval_jaxpr/qhr,kr->qhk/dot_general | solution.py:27
  60.2 4.7 %fusion.60 = (bf16[64,32,512]{2,0,1:T(8,128)(2,1)}, f32[64,32]{0,1:T(8,128)S(1)}) fusion(f32[512,64,32]{0,1,2:T(8,128)} %get-tuple-element.220, f32[64,32]{0,1:T(8,128)S(1)} %select_maximum_fusion.2, pred[64,512]{1,0:T(8,128)(4,1)S(1)} %broadcast_compare_fusion.2), kind=kLoop, calls=%fused_computation.9.clone.1 | loop fusion | flops 4192256 | bytes 6340608 | tf_op jit(solution)/shard_map/while/body/eval_jaxpr/convert_element_type | solution.py:36
  64.9 0.1 copy.79
  65.0 5.6 %fusion.62 = f32[64,32,512]{2,1,0:T(8,128)} fusion(f32[64,32,512]{2,1,0:T(8,128)} %get-tuple-element.240, bf16[64,32,512]{2,0,1:T(8,128)(2,1)} %get-tuple-element.223, f32[64,32]{1,0:T(8,128)S(1)} %copy.79, pred[]{:T(512)S(6)} %compare.11, bf16[2,512,512]{2,1,0:T(8,128)(2,1)S(1)} %get-tuple-element.254, s32[]{:T(128)} %get-tuple-element.237), kind=kOutput, calls=%fused_computation.7.clone.1 | convolution fusion | flops 1076887552 | bytes 11042821 | tf_op jit(solution)/shard_map/while/body/eval_jaxpr/qhk,kl->qhl/dot_general | solution.py:35
  70.5 2.9 %fusion.58 = f32[512,64,32]{0,1,2:T(8,128)S(1)} fusion(bf16[64,32,512]{2,0,1:T(8,128)(2,1)} %get-tuple-element.255, bf16[2,512,512]{2,1,0:T(8,128)(2,1)S(1)} %get-tuple-element.254, s32[]{:T(128)} %get-tuple-element.237), kind=kOutput, calls=%fused_computation.13.clone.1 | convolution fusion | flops 1073741824 | bytes 6815748 | tf_op jit(solution)/shard_map/while/body/eval_jaxpr/qhl,kl->qhk/dot_general | solution.py:25
  73.5 0.1 broadcast_compare_fusion.2
  73.6 0.0 copy-done.2
  73.6 2.9 %fusion.59 = (f32[64,32]{0,1:T(8,128)S(1)}, f32[512,64,32]{0,1,2:T(8,128)}) fusion(pred[64,512]{1,0:T(8,128)(4,1)S(1)} %broadcast_compare_fusion.2, f32[512,64,32]{0,1,2:T(8,128)S(1)} %fusion.58, bf16[64,32,64]{2,0,1:T(8,128)(2,1)S(1)} %get-tuple-element.257, bf16[2,512,64]{1,2,0:T(8,128)(2,1)S(1)} %copy-done.2, s32[]{:T(128)} %get-tuple-element.237), kind=kOutput, calls=%fused_computation.3.clone.1 | convolution fusion | flops 138409984 | bytes 9019396 | tf_op jit(solution)/shard_map/while/body/eval_jaxpr/qhr,kr->qhk/dot_general | solution.py:27
  76.5 4.7 %fusion.60 = (bf16[64,32,512]{2,0,1:T(8,128)(2,1)}, f32[64,32]{0,1:T(8,128)S(1)}) fusion(f32[512,64,32]{0,1,2:T(8,128)} %get-tuple-element.220, f32[64,32]{0,1:T(8,128)S(1)} %select_maximum_fusion.2, pred[64,512]{1,0:T(8,128)(4,1)S(1)} %broadcast_compare_fusion.2), kind=kLoop, calls=%fused_computation.9.clone.1 | loop fusion | flops 4192256 | bytes 6340608 | tf_op jit(solution)/shard_map/while/body/eval_jaxpr/convert_element_type | solution.py:36
  81.2 0.1 copy.79
  81.3 6.8 %fusion.62 = f32[64,32,512]{2,1,0:T(8,128)} fusion(f32[64,32,512]{2,1,0:T(8,128)} %get-tuple-element.240, bf16[64,32,512]{2,0,1:T(8,128)(2,1)} %get-tuple-element.223, f32[64,32]{1,0:T(8,128)S(1)} %copy.79, pred[]{:T(512)S(6)} %compare.11, bf16[2,512,512]{2,1,0:T(8,128)(2,1)S(1)} %get-tuple-element.254, s32[]{:T(128)} %get-tuple-element.237), kind=kOutput, calls=%fused_computation.7.clone.1 | convolution fusion | flops 1076887552 | bytes 11042821 | tf_op jit(solution)/shard_map/while/body/eval_jaxpr/qhk,kl->qhl/dot_general | solution.py:35
  88.1 0.1 copy.43
  88.1 2.7 %divide_convert_fusion = bf16[64,32,512]{2,1,0:T(8,128)(2,1)S(1)} fusion(f32[64,32,512]{2,1,0:T(8,128)} %get-tuple-element.58, f32[64,32]{1,0:T(8,128)S(1)} %copy.43), kind=kLoop, calls=%fused_computation.34 | loop fusion | flops 2097152 | bytes 6299648 | tf_op jit(solution)/shard_map/convert_element_type | solution.py:114
  90.9 0.7 copy-done.1
  91.6 2.5 %fusion.31 = bf16[32,8,8,128]{3,2,1,0:T(8,128)(2,1)S(1)} fusion(bf16[32,512,128]{2,1,0:T(8,128)(2,1)S(1)} %copy-done.1, bf16[64,32,512]{2,1,0:T(8,128)(2,1)S(1)} %divide_convert_fusion), kind=kOutput, calls=%fused_computation.43 | convolution fusion | flops 268697600 | bytes 6815744 | tf_op jit(solution)/shard_map/qhl,hlv->qhv/dot_general | solution.py:115
  94.1 0.9 copy.75
  95.1 0.0 all-gather.5.cloned.1.call-update
  95.1 0.0 copy-start.3
  95.1 0.2 all-reduce.3.cloned.1.call-start
  95.3 73.6 %all-gather.5.cloned.1.call-done = bf16[1024,4096]{1,0:T(8,128)(2,1)} async-done(((bf16[64,4096]{1,0:T(8,128)(2,1)}), bf16[1024,4096]{1,0:T(8,128)(2,1)}) %all-gather.5.cloned.1.call-update) | async-done | bytes 8388624 | tf_op jit(solution)/shard_map/all_gather | solution.py:118
  168.9 0.0 copy-done
  168.9 6.0 %fusion.28 = bf16[1024,224]{0,1:T(8,128)(2,1)S(1)} fusion(bf16[1024,4096]{1,0:T(8,128)(2,1)} %all-gather.5.cloned.1.call-done, bf16[32,128,224]{1,2,0:T(8,128)(2,1)S(1)} %copy-done), kind=kOutput, calls=%fused_computation.42 | convolution fusion | flops 1879277568 | bytes 10682368 | tf_op jit(solution)/shard_map/qk,kd->qd/dot_general | solution.py:119
  175.0 1.0 copy.47
  176.0 0.0 all-reduce.3.cloned.1.call-update
  176.0 0.0 copy-done.3
  176.0 0.6 dynamic-slice
  176.6 26.4 %all-reduce.3.cloned.1.call-done = bf16[16,2,32,224]{3,2,1,0:T(8,128)(2,1)} async-done(((bf16[16,2,32,224]{3,2,1,0:T(8,128)(2,1)}), bf16[16,2,32,224]{3,2,1,0:T(8,128)(2,1)}) %all-reduce.3.cloned.1.call-update) | async-done | bytes 458768
  203.0 1.6 dynamic-slice_bitcast_fusion
  204.6 15.5 %all_to_all.5 = bf16[16,32,224]{2,1,0:T(8,128)(2,1)S(1)} all-to-all(bf16[16,32,224]{2,1,0:T(8,128)(2,1)S(1)} %dynamic-slice_bitcast_fusion), channel_id=1, replica_groups=mesh['ctx'=16,'head'=2] {'ctx'}, dimensions={0} | all-to-all | bytes 458752 | tf_op jit(solution)/shard_map/all_to_all | solution.py:129
  220.1 0.1 copy.48
  220.3 1.0 reshape.74
  (16 shorter events, 0.1 us)
Async XLA Ops:
  6.5 162.4 %copy-start = (bf16[32,128,224]{1,2,0:T(8,128)(2,1)S(1)}, bf16[32,128,224]{1,2,0:T(8,128)(2,1)}, u32[]{:S(2)}) copy-start(bf16[32,128,224]{1,2,0:T(8,128)(2,1)} %param.15) | copy-start | bytes 5505028
  6.5 44.6 %all-gather.3.cloned.1.call-start = ((), (), s32[]{:S(2)}) async-start(), calls=%async_computation.1 | async-start | bytes 1392640 | tf_op jit(solution)/shard_map/all_gather | solution.py:103
  8.2 160.8 %all-gather.5.cloned.1.call-start = ((), (), s32[]{:S(2)}) async-start(), calls=%async_computation.2 | async-start | bytes 8912896 | tf_op jit(solution)/shard_map/all_gather | solution.py:118
  54.2 3.1 %copy-start.2 = (bf16[2,512,64]{1,2,0:T(8,128)(2,1)S(1)}, bf16[2,512,64]{1,2,0:T(8,128)(2,1)}, u32[]{:S(2)}) copy-start(bf16[2,512,64]{1,2,0:T(8,128)(2,1)} %get-tuple-element.256) | copy-start | bytes 393220 | tf_op jit(solution)/shard_map/while
  70.5 3.1 %copy-start.2 = (bf16[2,512,64]{1,2,0:T(8,128)(2,1)S(1)}, bf16[2,512,64]{1,2,0:T(8,128)(2,1)}, u32[]{:S(2)}) copy-start(bf16[2,512,64]{1,2,0:T(8,128)(2,1)} %get-tuple-element.256) | copy-start | bytes 393220 | tf_op jit(solution)/shard_map/while
  88.1 3.5 %copy-start.1 = (bf16[32,512,128]{2,1,0:T(8,128)(2,1)S(1)}, bf16[32,512,128]{2,1,0:T(8,128)(2,1)}, u32[]{:S(2)}) copy-start(bf16[32,512,128]{2,1,0:T(8,128)(2,1)} %param.14) | copy-start | bytes 12582916
  95.1 80.9 %copy-start.3 = (u32[32]{0:T(128)S(1)}, u32[32]{0:T(128)}, u32[]{:S(2)}) copy-start(u32[32]{0:T(128)} %constant.94) | copy-start | bytes 388
  95.1 107.9 %all-reduce.3.cloned.1.call-start = ((), (), s32[]{:S(2)}) async-start(), calls=%async_computation.3 | async-start | bytes 1048576
Sparse Core Ops, SparseCore 0:
  9.6 41.4 all-gather.2
  95.2 73.7 all-gather.4
  176.1 26.8 all-reduce.2

commit v2 on v0

v2 whole, which is shorter than its diff:
```python
import functools
import math

import jax
import jax.numpy as jnp
from jax import lax
from jax.experimental import pallas as pl
from jax.experimental.pallas import tpu as pltpu
from jax.sharding import PartitionSpec as P

NOPE = 128
ROPE = 64
GROUPS = 4
KEY_STEP = 256
MESH = pl.DeviceIdType.MESH


def remote(src, dst, send_sem, recv_sem, device):
    return pltpu.make_async_remote_copy(
        src_ref=src,
        dst_ref=dst,
        send_sem=send_sem,
        recv_sem=recv_sem,
        device_id=device,
        device_id_type=MESH,
    )


def each(start, stop, body):
    def step(index, carry):
        body(index)
        return carry

    lax.fori_loop(start, stop, step, 0)


def kernel(
    n_ctx,
    n_head,
    q_ref,
    qr_ref,
    lat_ref,
    kr_ref,
    wuk_hbm,
    wuv_hbm,
    wo_hbm,
    out_ref,
    wuk,
    wuv,
    wo,
    blocks,
    keys,
    queries,
    latent_out,
    heads,
    part_out,
    part_in,
    summed,
    owned,
    load_sem,
    w_send,
    w_recv,
    k_recv,
    k_send_z,
    k_send_y,
    k_send_s,
    h_recv,
    h_send_z,
    h_send_s,
    p_send,
    p_recv,
    o_send,
    o_recv,
):
    rows = lat_ref.shape[0]
    half = rows // 2
    lat_dim = lat_ref.shape[1]
    heads_here = wuk_hbm.shape[0]
    line = n_ctx // 4
    me = lax.axis_index("ctx")
    group = lax.axis_index("head")
    a = me // 4
    b = (me // 2) % 2
    core = me % 2

    def dev(a_at, b_at, core_at):
        return (4 * a_at + 2 * b_at + core_at, group)

    def slot_dev(slot):
        return dev(slot // 2, b, slot % 2)

    slot_me = 2 * a + core
    slots = 2 * line

    load_uk = pltpu.make_async_copy(wuk_hbm, wuk, load_sem.at[0])
    load_uv = pltpu.make_async_copy(wuv_hbm, wuv, load_sem.at[1])
    load_wo = pltpu.make_async_copy(wo_hbm, wo.at[b], load_sem.at[2])
    load_uk.start()
    load_uv.start()
    load_wo.start()

    blocks[me, :, :lat_dim] = lat_ref[...]
    blocks[me, :, lat_dim : lat_dim + ROPE] = kr_ref[...]
    blocks[me, :, lat_dim + ROPE :] = jnp.zeros((rows, 128 - ROPE), jnp.bfloat16)

    barrier = pltpu.get_barrier_semaphore()

    def greet(step):
        other = lax.rem(slot_me + step, slots)
        pl.semaphore_signal(barrier, inc=1, device_id=slot_dev(other), device_id_type=MESH)

    each(1, slots, greet)
    pl.semaphore_signal(barrier, inc=1, device_id=dev(a, 1 - b, core), device_id_type=MESH)
    for step in range(1, n_head):
        pl.semaphore_signal(
            barrier,
            inc=1,
            device_id=(me, lax.rem(group + step, n_head)),
            device_id_type=MESH,
        )
    pl.semaphore_wait(barrier, slots - 1 + 1 + n_head - 1)

    def key_block(src_a, src_b):
        return 4 * src_a + 2 * src_b + core

    def key_copy(index, send_sem, device):
        return remote(blocks.at[index], blocks.at[index], send_sem, k_recv.at[index], device)

    def key_right(src):
        return key_copy(key_block(src, b), k_send_z.at[src], dev(a + 1, b, core))

    def key_left(src, sem):
        return key_copy(key_block(src, b), k_send_z.at[sem], dev(a - 1, b, core))

    def key_y(src):
        return key_copy(key_block(src, b), k_send_y.at[src], dev(a, 1 - b, core))

    def key_s(src, src_b):
        return key_copy(key_block(src, src_b), k_send_s.at[src_b, src], dev(a, b, 1 - core))

    @pl.when(a < line - 1)
    def _():
        key_right(a).start()

    @pl.when(a > 0)
    def _():
        key_left(a, line).start()

    key_y(a).start()
    key_s(a, b).start()

    def relay_keys(k):
        @pl.when(a - k >= 0)
        def _():
            src = a - k
            key_s(src, b).wait_recv()

            @pl.when(a < line - 1)
            def _():
                key_right(src).start()

            key_y(src).start()
            key_s(src, b).start()

        @pl.when(a + k < line)
        def _():
            src = a + k
            key_s(src, b).wait_recv()

            @pl.when(a > 0)
            def _():
                key_left(src, src).start()

            key_y(src).start()
            key_s(src, b).start()

    heads_group = heads_here // GROUPS
    load_uk.wait()
    for g in range(GROUPS):

        def query_pair(p):
            rope = qr_ref[:, pl.ds(pl.multiple_of(p * 2 * ROPE, 2 * ROPE), 2 * ROPE)]
            for odd in range(2):
                h = 2 * p + odd
                q = q_ref[:, pl.ds(pl.multiple_of(h * NOPE, NOPE), NOPE)]
                ql = jnp.dot(q, wuk[h], preferred_element_type=jnp.float32).astype(jnp.bfloat16)
                tail = rope[:, odd * ROPE : (odd + 1) * ROPE]
                tail = jnp.concatenate([tail, jnp.zeros_like(tail)], axis=1)
                for part in range(2):
                    at = pl.ds(pl.multiple_of(h * half, half), half)
                    queries[part, at, :lat_dim] = ql[part * half : (part + 1) * half]
                    queries[part, at, lat_dim:] = tail[part * half : (part + 1) * half]

        each(g * heads_group // 2, (g + 1) * heads_group // 2, query_pair)
        each(
            1 + -(-g * (line - 1) // GROUPS),
            1 + -(-(g + 1) * (line - 1) // GROUPS),
            relay_keys,
        )

    def far_keys(src):
        key_s(src, 1 - b).wait_recv()
        key_s(src, 1 - b).start()

    each(0, line, far_keys)

    depth = wo_hbm.shape[0] // GROUPS

    def weight_copy(g, owner):
        at = pl.ds(pl.multiple_of(g * depth, depth), depth)
        return remote(
            wo_hbm.at[at],
            wo.at[owner, at],
            w_send.at[g],
            w_recv.at[g],
            dev(a, 1 - b, core),
        )

    for g in range(GROUPS):
        weight_copy(g, b).start()

    def near_keys(src):
        for src_b in range(2):
            index = 4 * src + 2 * src_b + (1 - core)
            remote(
                blocks.at[index],
                blocks.at[index],
                k_send_s.at[src_b, src],
                k_recv.at[index],
                dev(a, b, 1 - core),
            ).wait_recv()

    each(0, line, near_keys)

    def place_keys(c):
        low = pl.ds(pl.multiple_of(c * half, half), half)
        high = pl.ds(pl.multiple_of((2 * n_ctx - 1 - c) * half, half), half)
        keys[low] = blocks[c, :half]
        keys[high] = blocks[c, half:]

    each(0, n_ctx, place_keys)

    def head_copy(src_core, src, g, send_sem, device):
        return remote(
            heads.at[src_core, src, g],
            heads.at[src_core, src, g],
            send_sem,
            h_recv.at[src_core, src, g],
            device,
        )

    def head_right(src, g):
        return head_copy(core, src, g, h_send_z.at[src, g], dev(a + 1, b, core))

    def head_left(src, g, sem):
        return head_copy(core, src, g, h_send_z.at[sem, g], dev(a - 1, b, core))

    def head_s(src, g):
        return head_copy(core, src, g, h_send_s.at[src, g], dev(a, b, 1 - core))

    scale = (NOPE + ROPE) ** -0.5 * math.log2(math.e)
    group_rows = heads_group * half
    steps = 2 * n_ctx * half // KEY_STEP

    def attend(g, part, base, count):
        length = count * KEY_STEP
        q = queries[part, pl.ds(pl.multiple_of(g * group_rows, group_rows), group_rows)]
        scores = lax.dot_general(
            q,
            keys[:length],
            (((1,), (1,)), ((), ())),
            preferred_element_type=jnp.float32,
        )
        shape = (group_rows, KEY_STEP)
        row = lax.rem(lax.broadcasted_iota(jnp.int32, shape, 0), half)
        column = lax.broadcasted_iota(jnp.int32, shape, 1)
        visible = column - row <= base - (length - KEY_STEP)
        last = jnp.where(visible, scores[:, length - KEY_STEP :], -jnp.inf)
        if count > 1:
            scores = jnp.concatenate([scores[:, : length - KEY_STEP], last], axis=1)
        else:
            scores = last
        best = jnp.max(scores, axis=1, keepdims=True)
        weights = jnp.exp2((scores - best) * scale)
        total = jnp.sum(weights, axis=1, keepdims=True)
        accum = jnp.dot(
            weights.astype(jnp.bfloat16),
            keys[:length, :lat_dim],
            preferred_element_type=jnp.float32,
        )
        latent_out[part] = (accum / total).astype(jnp.bfloat16)

    load_uv.wait()

    def attend_group(g):
        for part in range(2):
            base = me * half if part == 0 else (2 * n_ctx - 1 - me) * half
            need = base // KEY_STEP + 1
            for count in range(1, steps + 1):
                if (count <= (steps + 1) // 2) if part == 0 else (count >= steps // 2):

                    @pl.when(need == count)
                    def _():
                        attend(g, part, base, count)

        for i in range(heads_group):
            h = g * heads_group + i
            rows_at = slice(i * half, (i + 1) * half)
            lhs = jnp.concatenate([latent_out[0, rows_at], latent_out[1, rows_at]], axis=0)
            head = jnp.dot(lhs, wuv[h], preferred_element_type=jnp.float32)
            heads[core, a, g, :, i * 128 : (i + 1) * 128] = head.astype(jnp.bfloat16)

        @pl.when(a < line - 1)
        def _():
            head_right(a, g).start()

        @pl.when(a > 0)
        def _():
            head_left(a, g, line).start()

        head_s(a, g).start()

    each(0, GROUPS, attend_group)

    def relay_heads(k):
        def one(g):
            @pl.when(a - k >= 0)
            def _():
                src = a - k
                head_s(src, g).wait_recv()

                @pl.when(a < line - 1)
                def _():
                    head_right(src, g).start()

                head_s(src, g).start()

            @pl.when(a + k < line)
            def _():
                src = a + k
                head_s(src, g).wait_recv()

                @pl.when(a > 0)
                def _():
                    head_left(src, g, src).start()

                head_s(src, g).start()

        each(0, GROUPS, one)

    each(1, line, relay_heads)

    def near_heads(src):
        for g in range(GROUPS):
            head_copy(1 - core, src, g, h_send_s.at[src, g], dev(a, b, 1 - core)).wait_recv()

    each(0, line, near_heads)

    own_rows = rows // n_head
    cols = wo.shape[2]

    def part_copy(target, owner):
        return remote(
            part_out.at[target, owner],
            part_in.at[group, owner],
            p_send.at[target, owner],
            p_recv.at[group, owner],
            (me, target),
        )

    def part_arrival(source, owner):
        return remote(
            part_out.at[source, owner],
            part_in.at[source, owner],
            p_send.at[source, owner],
            p_recv.at[source, owner],
            (me, source),
        )

    def project(owner):
        total = jnp.zeros((slots * rows, cols), jnp.float32)
        for g in range(GROUPS):
            lhs = heads[:, :, g].reshape(slots * rows, depth)
            total = total + jnp.dot(
                lhs, wo[owner, g * depth : (g + 1) * depth], preferred_element_type=jnp.float32
            )
        total = total.reshape(slots, rows, cols)
        for target in range(n_head):
            part_out[target, owner] = total[
                :, target * own_rows : (target + 1) * own_rows
            ].astype(jnp.bfloat16)
        for step in range(1, n_head):
            part_copy(lax.rem(group + step, n_head), owner).start()

    load_wo.wait()
    project(b)
    for g in range(GROUPS):
        weight_copy(g, 1 - b).wait_recv()
    project(1 - b)

    for owner in (b, 1 - b):
        total = part_out[group, owner].astype(jnp.float32)
        for step in range(1, n_head):
            source = lax.rem(group + step, n_head)
            part_arrival(source, owner).wait_recv()
            total = total + part_in[source, owner].astype(jnp.float32)
        total = total.astype(jnp.bfloat16)
        for half_core in range(2):
            for at in range(line):
                summed[2 * at + half_core, owner] = total[half_core * line + at]

    def owned_copy(slot):
        return remote(
            summed.at[slot],
            owned.at[slot_me],
            o_send.at[slot],
            o_recv.at[slot_me],
            slot_dev(slot),
        )

    def owned_arrival(slot):
        return remote(
            summed.at[slot],
            owned.at[slot],
            o_send.at[slot],
            o_recv.at[slot],
            slot_dev(slot),
        )

    each(1, slots, lambda step: owned_copy(lax.rem(slot_me + step, slots)).start())
    owned[slot_me] = summed[slot_me]

    def key_sends(src):
        @pl.when(jnp.logical_or(jnp.logical_and(src <= a, a < line - 1), jnp.logical_and(src > a, a > 0)))
        def _():
            key_right(src).wait_send()
            for g in range(GROUPS):
                head_right(src, g).wait_send()

        key_y(src).wait_send()
        for src_b in range(2):
            key_s(src, src_b).wait_send()
        for g in range(GROUPS):
            head_s(src, g).wait_send()

    each(0, line, key_sends)

    @pl.when(a > 0)
    def _():
        key_left(a, line).wait_send()
        for g in range(GROUPS):
            head_left(a, g, line).wait_send()

    for g in range(GROUPS):
        weight_copy(g, b).wait_send()
    for step in range(1, n_head):
        for owner in range(2):
            part_copy(lax.rem(group + step, n_head), owner).wait_send()

    each(1, slots, lambda step: owned_arrival(lax.rem(slot_me + step, slots)).wait_recv())
    each(1, slots, lambda step: owned_copy(lax.rem(slot_me + step, slots)).wait_send())
    out_ref[...] = jnp.concatenate(
        [owned[2 * (c // 4) + c % 2, (c // 2) % 2] for c in range(n_ctx)], axis=1
    )


def shards(q_nope, query_rope, latent, key_rope, w_uk, w_uv, w_out):
    rows, lat_dim = latent.shape
    n_ctx = lax.axis_size("ctx")
    n_head = lax.axis_size("head")
    heads_here = w_uk.shape[0]
    value_dim = w_uv.shape[2]
    cols = w_out.shape[2]
    line = n_ctx // 4
    slots = 2 * line
    own_rows = rows // n_head
    group_width = heads_here // GROUPS * value_dim
    wide = lat_dim + 128
    bf16 = jnp.bfloat16
    dma = pltpu.SemaphoreType.DMA
    vmem = pl.BlockSpec(memory_space=pltpu.VMEM)
    anywhere = pl.BlockSpec(memory_space=pl.ANY)
    return pl.pallas_call(
        functools.partial(kernel, n_ctx, n_head),
        out_shape=jax.ShapeDtypeStruct((own_rows, n_ctx * cols), bf16),
        in_specs=[vmem] * 4 + [anywhere] * 3,
        out_specs=vmem,
        scratch_shapes=[
            pltpu.VMEM(w_uk.shape, bf16),
            pltpu.VMEM(w_uv.shape, bf16),
            pltpu.VMEM((2, heads_here * value_dim, cols), bf16),
            pltpu.VMEM((n_ctx, rows, wide), bf16),
            pltpu.VMEM((n_ctx * rows, wide), bf16),
            pltpu.VMEM((2, heads_here * rows // 2, wide), bf16),
            pltpu.VMEM((2, heads_here // GROUPS * rows // 2, lat_dim), bf16),
            pltpu.VMEM((2, line, GROUPS, rows, group_width), bf16),
            pltpu.VMEM((n_head, 2, slots, own_rows, cols), bf16),
            pltpu.VMEM((n_head, 2, slots, own_rows, cols), bf16),
            pltpu.VMEM((slots, 2, own_rows, cols), bf16),
            pltpu.VMEM((slots, 2, own_rows, cols), bf16),
            dma((3,)),
            dma((GROUPS,)),
            dma((GROUPS,)),
            dma((n_ctx,)),
            dma((line + 1,)),
            dma((line,)),
            dma((2, line)),
            dma((2, line, GROUPS)),
            dma((line + 1, GROUPS)),
            dma((line, GROUPS)),
            dma((n_head, 2)),
            dma((n_head, 2)),
            dma((slots,)),
            dma((slots,)),
        ],
        compiler_params=pltpu.CompilerParams(
            collective_id=0, has_side_effects=True, vmem_limit_bytes=56 * 1024 * 1024
        ),
    )(
        q_nope,
        query_rope,
        latent,
        key_rope,
        w_uk,
        w_uv,
        w_out.reshape(heads_here * value_dim, cols),
    )


def solution(mesh):
    placed = (
        P("ctx", "head"),
        P("ctx", "head"),
        P("ctx", None),
        P("ctx", None),
        P("head", None, None),
        P("head", None, None),
        P("head", None, "ctx"),
    )
    return jax.shard_map(
        shards, mesh=mesh, in_specs=placed, out_specs=P(("ctx", "head"), None), check_vma=False
    )
```

time: 237 us -> 83.9 us (0.35)
  waiting for transfers between devices: 141 us -> 0 us
  Pallas kernels: 0 us -> 78 us
  matrix products: 45 us -> 0 us
  blocking collectives: 24.3 us -> 0 us
  between operations: 13.2 us -> 0.01 us
  other arithmetic: 10.9 us -> 0 us
  local copies, waits for them, and re-layouts: 2.08 us -> 5.61 us
    all_gather x2 -> x0, waiting for transfers between devices: 126 us -> none  [the longest x1 114 us: shards(): lax.all_gather(w_out, 'ctx', axis=2, tiled=True)]
    pallas_call x0 -> x1, Pallas kernels: none -> 78 us  [shards(): pl.pallas_call(functools.partial(kernel, n_ctx, n_head), out_shape=jax.Sh...]
    dot_general x8 -> x0, matrix products: 45 us -> none  [the longest x1 17.4 us: shards(): jnp.einsum('qhv,hvd->qd', head_out, lax.all_gather(w_out, 'ctx', axis=2,...]
    all_gather x1 -> x0, blocking collectives: 24.3 us -> none  [shards(): lax.all_gather(key_rope, 'ctx', axis=0, tiled=True)]
    reduce_scatter x1 -> x0, waiting for transfers between devices: 14 us -> none  [shards(): lax.psum_scatter(partial_sum.astype(jnp.bfloat16), 'head', scatter_dimens...]
    convert_element_type x3 -> x0, other arithmetic: 10.6 us -> none  [the longest x2 8.09 us: attend_block(): weights.astype(jnp.bfloat16)]
    unnamed x4 -> x2, local copies, waits for them, and re-layouts: 0.34 us -> 5.61 us
  transfers between devices with their start and end apart: 3 -> 0, of which waited for: 3 -> 0; matrix products, arithmetic and copies ran while one was open for 17% -> 0% of each run, Pallas kernels for 0% -> 0%
where the time goes in v2:
time: 83.9 us; the launch traced here: 83.7 us
  Pallas kernels  78 us (93%)
  local copies, waits for them, and re-layouts  5.61 us (7%)
    pallas_call x1, Pallas kernels, shards(): pl.pallas_call(functools.partial(kernel, n_ctx, n_head), out_shape=jax.Sh...  78 us
    unnamed x2, local copies, waits for them, and re-layouts  5.61 us

profile of v2, /device:TPU:0, one launch (start us, length us, event | category | flops | bytes accessed | tf_op | source)
XLA Modules:
  0.0 83.7 jit_solution(3926645021127918491)
XLA Ops:
  0.0 4.0 %copy.8 = bf16[32,128,224]{2,1,0:T(8,128)(2,1)} copy(bf16[32,128,224]{1,2,0:T(8,128)(2,1)} %param.13) | data formatting | bytes 3670016 | tf_op args[6]
  4.0 78.0 %shard_map.73 = bf16[32,3584]{1,0:T(8,128)(2,1)} custom-call(bf16[64,4096]{1,0:T(8,128)(2,1)} %q_ref.1, bf16[64,2048]{1,0:T(8,128)(2,1)} %qr_ref.1, bf16[64,512]{1,0:T(8,128)(2,1)} %lat_ref.1, bf16[64,64]{1,0:T(8,128)(2,1)} %kr_ref.1, bf16[32,128,512]{2,1,0:T(8,128)(2,1)} %wuk_hbm.1, bf16[32,512,128]{2,1,0:T(8,128)(2,1)} %wuv_hbm.1, bf16[4096,224]{1,0:T(8,128)(2,1)} %bitcast.1), custom_call_target="tpu_custom_call" | custom-call | tf_op jit(solution)/shard_map/pallas_call | solution.py:483
  82.0 1.6 %copy.10 = bf16[32,3584]{1,0:T(8,128)(2,1)} copy(bf16[32,3584]{1,0:T(8,128)(2,1)} %shard_map.73) | data formatting | bytes 458752

commit v3 on v2

--- a/solution.py
+++ b/solution.py
@@ -11,6 +11,7 @@
 NOPE = 128
 ROPE = 64
 GROUPS = 4
+CHUNKS = 8
 KEY_STEP = 256
 MESH = pl.DeviceIdType.MESH
 
@@ -47,6 +48,7 @@
     out_ref,
     wuk,
     wuv,
+    wt,
     wo,
     blocks,
     keys,
@@ -94,7 +96,7 @@
 
     load_uk = pltpu.make_async_copy(wuk_hbm, wuk, load_sem.at[0])
     load_uv = pltpu.make_async_copy(wuv_hbm, wuv, load_sem.at[1])
-    load_wo = pltpu.make_async_copy(wo_hbm, wo.at[b], load_sem.at[2])
+    load_wo = pltpu.make_async_copy(wo_hbm, wt.at[b], load_sem.at[2])
     load_uk.start()
     load_uv.start()
     load_wo.start()
@@ -148,6 +150,20 @@
 
     key_y(a).start()
     key_s(a, b).start()
+
+    depth = heads_here // CHUNKS
+
+    def weight_copy(chunk, owner):
+        at = pl.ds(chunk * depth, depth)
+        return remote(
+            wo_hbm.at[at],
+            wt.at[owner, at],
+            w_send.at[chunk],
+            w_recv.at[chunk],
+            dev(a, 1 - b, core),
+        )
+
+    weight_copy(0, b).start()
 
     def relay_keys(k):
         @pl.when(a - k >= 0)
@@ -198,26 +214,13 @@
             relay_keys,
         )
 
+    each(1, CHUNKS, lambda chunk: weight_copy(chunk, b).start())
+
     def far_keys(src):
         key_s(src, 1 - b).wait_recv()
         key_s(src, 1 - b).start()
 
     each(0, line, far_keys)
-
-    depth = wo_hbm.shape[0] // GROUPS
-
-    def weight_copy(g, owner):
-        at = pl.ds(pl.multiple_of(g * depth, depth), depth)
-        return remote(
-            wo_hbm.at[at],
-            wo.at[owner, at],
-            w_send.at[g],
-            w_recv.at[g],
-            dev(a, 1 - b, core),
-        )
-
-    for g in range(GROUPS):
-        weight_copy(g, b).start()
 
     def near_keys(src):
         for src_b in range(2):
@@ -230,6 +233,16 @@
                 dev(a, b, 1 - core),
             ).wait_recv()
 
+    value_dim = wt.shape[3]
+
+    def turn(owner):
+        def one(h):
+            wo[owner, pl.ds(pl.multiple_of(h * value_dim, value_dim), value_dim)] = wt[owner, h].T
+
+        each(0, heads_here, one)
+
+    load_wo.wait()
+    turn(b)
     each(0, line, near_keys)
 
     def place_keys(c):
@@ -348,87 +361,132 @@
 
         each(0, GROUPS, one)
 
-    each(1, line, relay_heads)
+    own_rows = rows // n_head
+    cols = wo.shape[2]
+    width = heads_group * value_dim
+
+    def sides(k, body):
+        @pl.when(a - k >= 0)
+        def _():
+            body(a - k)
+
+        @pl.when(jnp.logical_and(k >= 1, a + k < line))
+        def _():
+            body(a + k)
+
+    def part_copy(target, owner, src):
+        return remote(
+            part_out.at[target, owner, src],
+            part_in.at[group, owner, src],
+            p_send.at[target, owner, src],
+            p_recv.at[group, owner, src],
+            (me, target),
+        )
+
+    def part_arrival(source, owner, src):
+        return remote(
+            part_out.at[source, owner, src],
+            part_in.at[source, owner, src],
+            p_send.at[source, owner, src],
+            p_recv.at[source, owner, src],
+            (me, source),
+        )
 
     def near_heads(src):
         for g in range(GROUPS):
             head_copy(1 - core, src, g, h_send_s.at[src, g], dev(a, b, 1 - core)).wait_recv()
 
-    each(0, line, near_heads)
-
-    own_rows = rows // n_head
-    cols = wo.shape[2]
-
-    def part_copy(target, owner):
-        return remote(
-            part_out.at[target, owner],
-            part_in.at[group, owner],
-            p_send.at[target, owner],
-            p_recv.at[group, owner],
-            (me, target),
-        )
-
-    def part_arrival(source, owner):
-        return remote(
-            part_out.at[source, owner],
-            part_in.at[source, owner],
-            p_send.at[source, owner],
-            p_recv.at[source, owner],
-            (me, source),
-        )
-
-    def project(owner):
-        total = jnp.zeros((slots * rows, cols), jnp.float32)
+    def project(src, owner):
+        total = jnp.zeros((2 * rows, cols), jnp.float32)
         for g in range(GROUPS):
-            lhs = heads[:, :, g].reshape(slots * rows, depth)
+            lhs = heads[:, src, g].reshape(2 * rows, width)
             total = total + jnp.dot(
-                lhs, wo[owner, g * depth : (g + 1) * depth], preferred_element_type=jnp.float32
+                lhs, wo[owner, g * width : (g + 1) * width], preferred_element_type=jnp.float32
             )
-        total = total.reshape(slots, rows, cols)
+        total = total.reshape(2, rows, cols)
         for target in range(n_head):
-            part_out[target, owner] = total[
+            part_out[target, owner, src] = total[
                 :, target * own_rows : (target + 1) * own_rows
             ].astype(jnp.bfloat16)
         for step in range(1, n_head):
-            part_copy(lax.rem(group + step, n_head), owner).start()
-
-    load_wo.wait()
-    project(b)
-    for g in range(GROUPS):
-        weight_copy(g, 1 - b).wait_recv()
-    project(1 - b)
-
-    for owner in (b, 1 - b):
-        total = part_out[group, owner].astype(jnp.float32)
+            part_copy(lax.rem(group + step, n_head), owner, src).start()
+
+    def owned_copy(slot, owner):
+        return remote(
+            summed.at[slot, owner],
+            owned.at[slot_me, owner],
+            o_send.at[slot, owner],
+            o_recv.at[slot_me, owner],
+            slot_dev(slot),
+        )
+
+    def owned_arrival(slot, owner):
+        return remote(
+            summed.at[slot, owner],
+            owned.at[slot, owner],
+            o_send.at[slot, owner],
+            o_recv.at[slot, owner],
+            slot_dev(slot),
+        )
+
+    def finish(src, owner):
+        total = part_out[group, owner, src].astype(jnp.float32)
         for step in range(1, n_head):
             source = lax.rem(group + step, n_head)
-            part_arrival(source, owner).wait_recv()
-            total = total + part_in[source, owner].astype(jnp.float32)
+            part_arrival(source, owner, src).wait_recv()
+            total = total + part_in[source, owner, src].astype(jnp.float32)
         total = total.astype(jnp.bfloat16)
-        for half_core in range(2):
-            for at in range(line):
-                summed[2 * at + half_core, owner] = total[half_core * line + at]
-
-    def owned_copy(slot):
-        return remote(
-            summed.at[slot],
-            owned.at[slot_me],
-            o_send.at[slot],
-            o_recv.at[slot_me],
-            slot_dev(slot),
-        )
-
-    def owned_arrival(slot):
-        return remote(
-            summed.at[slot],
-            owned.at[slot],
-            o_send.at[slot],
-            o_recv.at[slot],
-            slot_dev(slot),
-        )
-
-    each(1, slots, lambda step: owned_copy(lax.rem(slot_me + step, slots)).start())
-    owned[slot_me] = summed[slot_me]
+        for at in range(2):
+            slot = 2 * src + at
+            summed[slot, owner] = total[at]
+
+            @pl.when(slot != slot_me)
+            def _():
+                owned_copy(slot, owner).start()
+
+            @pl.when(slot == slot_me)
+            def _():
+                owned[slot_me, owner] = total[at]
+
+    def arrive_own(src):
+        near_heads(src)
+        project(src, b)
+
+    def far_step(k):
+        sides(k, lambda src: project(src, 1 - b))
+
+    def far_finish(k):
+        sides(k, lambda src: finish(src, 1 - b))
+
+    def near_step(k):
+        relay_heads(k + 1)
+        sides(k, arrive_own)
+
+        @pl.when(k >= 1)
+        def _():
+            sides(k - 1, lambda src: finish(src, b))
+
+    each(0, line - 2, near_step)
+    sides(line - 2, arrive_own)
+    sides(line - 3, lambda src: finish(src, b))
+    each(0, CHUNKS, lambda chunk: weight_copy(chunk, 1 - b).wait_recv())
+    turn(1 - b)
+    each(0, line - 1, far_step)
+    sides(line - 2, lambda src: finish(src, b))
+    each(0, line - 1, far_finish)
+    relay_heads(line - 1)
+
+    def arrive_last(src):
+        near_heads(src)
+        project(src, b)
+        project(src, 1 - b)
+
+    def finish_last(src):
+        finish(src, b)
+        finish(src, 1 - b)
+
+    sides(line - 1, arrive_last)
+    sides(line - 1, finish_last)
 
     def key_sends(src):
         @pl.when(jnp.logical_or(jnp.logical_and(src <= a, a < line - 1), jnp.logical_and(src > a, a > 0)))
@@ -451,14 +509,21 @@
         for g in range(GROUPS):
             head_left(a, g, line).wait_send()
 
-    for g in range(GROUPS):
-        weight_copy(g, b).wait_send()
-    for step in range(1, n_head):
+    each(0, CHUNKS, lambda chunk: weight_copy(chunk, b).wait_send())
+
+    def part_sends(src):
+        for step in range(1, n_head):
+            for owner in range(2):
+                part_copy(lax.rem(group + step, n_head), owner, src).wait_send()
+
+    each(0, line, part_sends)
+
+    def owned_waits(step):
         for owner in range(2):
-            part_copy(lax.rem(group + step, n_head), owner).wait_send()
-
-    each(1, slots, lambda step: owned_arrival(lax.rem(slot_me + step, slots)).wait_recv())
-    each(1, slots, lambda step: owned_copy(lax.rem(slot_me + step, slots)).wait_send())
+            owned_arrival(lax.rem(slot_me + step, slots), owner).wait_recv()
+            owned_copy(lax.rem(slot_me + step, slots), owner).wait_send()
+
+    each(1, slots, owned_waits)
     out_ref[...] = jnp.concatenate(
         [owned[2 * (c // 4) + c % 2, (c // 2) % 2] for c in range(n_ctx)], axis=1
     )
@@ -488,19 +553,20 @@
         scratch_shapes=[
             pltpu.VMEM(w_uk.shape, bf16),
             pltpu.VMEM(w_uv.shape, bf16),
+            pltpu.VMEM((2, heads_here, cols, value_dim), bf16),
             pltpu.VMEM((2, heads_here * value_dim, cols), bf16),
             pltpu.VMEM((n_ctx, rows, wide), bf16),
             pltpu.VMEM((n_ctx * rows, wide), bf16),
             pltpu.VMEM((2, heads_here * rows // 2, wide), bf16),
             pltpu.VMEM((2, heads_here // GROUPS * rows // 2, lat_dim), bf16),
             pltpu.VMEM((2, line, GROUPS, rows, group_width), bf16),
-            pltpu.VMEM((n_head, 2, slots, own_rows, cols), bf16),
-            pltpu.VMEM((n_head, 2, slots, own_rows, cols), bf16),
+            pltpu.VMEM((n_head, 2, line, 2, own_rows, cols), bf16),
+            pltpu.VMEM((n_head, 2, line, 2, own_rows, cols), bf16),
             pltpu.VMEM((slots, 2, own_rows, cols), bf16),
             pltpu.VMEM((slots, 2, own_rows, cols), bf16),
             dma((3,)),
-            dma((GROUPS,)),
-            dma((GROUPS,)),
+            dma((CHUNKS,)),
+            dma((CHUNKS,)),
             dma((n_ctx,)),
             dma((line + 1,)),
             dma((line,)),
@@ -508,10 +574,10 @@
             dma((2, line, GROUPS)),
             dma((line + 1, GROUPS)),
             dma((line, GROUPS)),
-            dma((n_head, 2)),
-            dma((n_head, 2)),
-            dma((slots,)),
-            dma((slots,)),
+            dma((n_head, 2, line)),
+            dma((n_head, 2, line)),
+            dma((slots, 2)),
+            dma((slots, 2)),
         ],
         compiler_params=pltpu.CompilerParams(
             collective_id=0, has_side_effects=True, vmem_limit_bytes=56 * 1024 * 1024
@@ -523,7 +589,7 @@
         key_rope,
         w_uk,
         w_uv,
-        w_out.reshape(heads_here * value_dim, cols),
+        w_out.transpose(0, 2, 1),
     )
 
 

time: 83.9 us -> 73.6 us (0.88)
  Pallas kernels: 78 us -> 71.8 us
  local copies, waits for them, and re-layouts: 5.61 us -> 1.64 us
    pallas_call x1, Pallas kernels: 78 us -> 71.8 us  [shards(): pl.pallas_call(functools.partial(kernel, n_ctx, n_head), out_shape=jax.Sh...]
    unnamed x2 -> x1, local copies, waits for them, and re-layouts: 5.61 us -> 1.64 us
where the time goes in v3:
time: 73.6 us; the launch traced here: 73.4 us
  Pallas kernels  71.8 us (98%)
  local copies, waits for them, and re-layouts  1.64 us (2%)
    pallas_call x1, Pallas kernels, shards(): pl.pallas_call(functools.partial(kernel, n_ctx, n_head), out_shape=jax.Sh...  71.8 us
    unnamed x1, local copies, waits for them, and re-layouts  1.64 us

profile of v3, /device:TPU:0, one launch (start us, length us, event | category | flops | bytes accessed | tf_op | source)
XLA Modules:
  0.0 73.4 jit_solution(16169962802555964521)
XLA Ops:
  0.0 71.8 %shard_map.73 = bf16[32,3584]{1,0:T(8,128)(2,1)} custom-call(bf16[64,4096]{1,0:T(8,128)(2,1)} %q_ref.1, bf16[64,2048]{1,0:T(8,128)(2,1)} %qr_ref.1, bf16[64,512]{1,0:T(8,128)(2,1)} %lat_ref.1, bf16[64,64]{1,0:T(8,128)(2,1)} %kr_ref.1, bf16[32,128,512]{2,1,0:T(8,128)(2,1)} %wuk_hbm.1, bf16[32,512,128]{2,1,0:T(8,128)(2,1)} %wuv_hbm.1, ...), custom_call_target="tpu_custom_call" | custom-call | tf_op jit(solution)/shard_map/pallas_call | solution.py:548
  71.8 1.6 %copy.9 = bf16[32,3584]{1,0:T(8,128)(2,1)} copy(bf16[32,3584]{1,0:T(8,128)(2,1)} %shard_map.73) | data formatting | bytes 458752
